TPU v7x, 32 devices: a whole 2x2x4 slice. The times are simulated.
32 devices in a mesh: grp: 2 (over y), rep: 4 (over x, core), tp: 4 (over z).
Axes of the slice: x: 2, y: 2, z: 4, core: 2. Of those that a mesh axis runs over, the one named last changes fastest.
Arguments:
- query: bfloat16 [512, 2, 8192], P(('grp', 'rep'), None, 'tp'), parts along dimension 0, may hold values from -8 to 8
- kv_pool: bfloat16 [2, 1280, 128, 8, 128], P(None, ('grp', 'rep'), None, 'tp'), parts along dimension 1, may hold values from -6 to 6, as said below
- ctx_len: int32 [512], P(('grp', 'rep')), parts along dimension 0, may hold values from 1 to 510, as said below
- migrations: int32 [8, 8, 3], P(('grp', 'rep')), parts along dimension 0, may hold values from 0 to 63, as said below
- o_weight: bfloat16 [8192, 8192], P('tp'), may hold values from -0.5 to 0.5
Outputs:
- layer_out: bfloat16 [512, 2, 8192], P(('grp', 'rep')), parts along dimension 0
- arrived_pages: bfloat16 [2, 256, 128, 8, 128], P(None, ('grp', 'rep'), None, 'tp'), parts along dimension 1
There are 2 independent parts, one for each index of `grp`. A program takes and returns all parts, laid end to end along the dimension named above; an argument that names none is the same for every part. Nothing has to cross between parts.
Inputs may be any that keep to these rules, and one draw needn't show every extreme that they name: For every replica, the page counts ceil((ctx_len + 2) / 128) of its 64 requests sum to at most 160, and its requests' pages lie in its pool in request order from its first page on. `migrations`: row q holds 8 entries (slot of a request on replica q, destination replica, pages moved). Half of the replicas each migrate 8 distinct requests, each with all its pages, which are exactly 4, to one destination among the other half, and each of those receives from exactly one replica; the rows of the other replicas are (0, q, 0) and they send nothing. `kv_pool`: head copies j and k hold equal values when j == k.
All inputs are finite; a program needn't handle non-finite values.
Results may differ from a plain program's by a relative error of at most 0.0054.
Values may be sent and summed in bfloat16 or wider, within the bound.
A program may use at most 512 MiB of HBM per device.

v0:
```python
import functools
import math

import jax
import jax.numpy as jnp
from jax import lax
from jax.experimental import pallas as pl
from jax.experimental.pallas import tpu as pltpu
from jax.sharding import PartitionSpec as P

MAXP = 4
MESH = pl.DeviceIdType.MESH
VMEM_BYTES = 60 * 1024 * 1024


def divisor_near(total, most):
    for parts in range(min(most, total), 0, -1):
        if total % parts == 0:
            return parts
    return 1


def gather_kernel(page_len, page_rows, ctx_ref, mig_ref, kv_ref, *refs):
    outs, (held, in_sems, out_sems) = refs[:2], refs[2:]
    entries = mig_ref.shape[1]
    span = MAXP * page_rows
    last = kv_ref.shape[1] - span

    def first_row(slot):
        def add(i, total):
            return total + (ctx_ref[i] + 2 + page_len - 1) // page_len

        return lax.fori_loop(0, slot, add, 0) * page_rows

    def fetch(c, e, row):
        return pltpu.make_async_copy(
            kv_ref.at[c, pl.ds(pl.multiple_of(row, page_rows), span)],
            held.at[c, e],
            in_sems.at[c, e],
        )

    def store(c, e):
        return pltpu.make_async_copy(
            held.at[c, e], outs[c].at[pl.ds(e * span, span)], out_sems.at[c, e]
        )

    for e in range(entries):
        row = jnp.minimum(first_row(mig_ref[0, e, 0]), last)
        for c in range(2):
            fetch(c, e, row).start()
    for e in range(entries):
        moves = mig_ref[0, e, 2] > 0
        for c in range(2):
            fetch(c, e, 0).wait()

            @pl.when(jnp.logical_not(moves))
            def _():
                held[c, e] = jnp.zeros((span, held.shape[3]), held.dtype)

            store(c, e).start()
    for e in range(entries):
        for c in range(2):
            store(c, e).wait()


def gather_pages(kv_rows, ctx_len, migrations, page_len, page_rows):
    entries = migrations.shape[1]
    hd = kv_rows.shape[2]
    span = MAXP * page_rows
    return pl.pallas_call(
        functools.partial(gather_kernel, page_len, page_rows),
        out_shape=[jax.ShapeDtypeStruct((entries * span, hd), kv_rows.dtype)] * 2,
        in_specs=[
            pl.BlockSpec(memory_space=pltpu.SMEM),
            pl.BlockSpec(memory_space=pltpu.SMEM),
            pl.BlockSpec(memory_space=pl.ANY),
        ],
        out_specs=[pl.BlockSpec(memory_space=pl.ANY)] * 2,
        scratch_shapes=[
            pltpu.VMEM((2, entries, span, hd), kv_rows.dtype),
            pltpu.SemaphoreType.DMA((2, entries)),
            pltpu.SemaphoreType.DMA((2, entries)),
        ],
        compiler_params=pltpu.CompilerParams(vmem_limit_bytes=VMEM_BYTES),
        name="gather_pages",
    )(ctx_len, migrations, kv_rows)


def attend_kernel(
    page_len, kv_slots, group, steps, chunks, together,
    ctx_ref, q_ref, kv_ref, out_ref, pool, starts, sems,
):
    requests, rows, hd = q_ref.shape
    page_rows = page_len * kv_slots
    pool_rows = kv_ref.shape[1]
    chunk_rows = pool_rows // chunks
    span = MAXP * page_rows
    last = pool_rows - span
    scale = 1.0 / math.sqrt(hd)

    def chunk_copy(c, i):
        part = pl.ds(pl.multiple_of(i * chunk_rows, chunk_rows), chunk_rows)
        return pltpu.make_async_copy(kv_ref.at[c, part], pool.at[c, part], sems.at[c, i])

    for i in range(chunks):
        for c in range(2):
            chunk_copy(c, i).start()

    def place(i, total):
        starts[i] = total
        return total + (ctx_ref[i] + 2 + page_len - 1) // page_len * page_rows

    lax.fori_loop(0, requests, place, 0)

    def wait_chunk(i, carry):
        for c in range(2):
            chunk_copy(c, i).wait()
        return carry

    row_id = lax.broadcasted_iota(jnp.int32, (rows, span), 0)
    column = lax.broadcasted_iota(jnp.int32, (rows, span), 1)
    per_step = kv_slots * group
    step_of = row_id // per_step
    same_head = (row_id % per_step) // group == column % kv_slots
    column = column - step_of * kv_slots

    def batch(b, waited):
        tail = jnp.minimum(starts[b * together + together - 1], last) + span
        needed = (tail + chunk_rows - 1) // chunk_rows
        lax.fori_loop(waited, needed, wait_chunk, 0)
        for u in range(together):
            r = b * together + u
            start = starts[r]
            base = pl.multiple_of(jnp.minimum(start, last), page_rows)
            low = start - base
            high = low + (ctx_ref[r] + 1) * kv_slots
            keys = pool[0, pl.ds(base, span), :]
            scores = lax.dot_general(
                q_ref[r], keys, (((1,), (1,)), ((), ())), preferred_element_type=jnp.float32
            ) * scale
            valid = same_head & (column + step_of * kv_slots >= low) & (column < high)
            scores = jnp.where(valid, scores, -1e30)
            top = jnp.max(scores, axis=1, keepdims=True)
            weights = jnp.exp(scores - top)
            total = jnp.sum(weights, axis=1, keepdims=True)
            values = pool[1, pl.ds(base, span), :]
            mixed = jnp.dot(
                weights.astype(jnp.bfloat16), values, preferred_element_type=jnp.float32
            )
            out_ref[r] = (mixed / total).astype(out_ref.dtype)
        return jnp.maximum(waited, needed)

    waited = lax.fori_loop(0, requests // together, batch, 0)
    lax.fori_loop(waited, chunks, wait_chunk, 0)


def attend(kv_rows, ctx_len, query, page_len, kv_slots):
    requests, steps, width = query.shape
    hd = kv_rows.shape[2]
    heads = width // hd
    group = heads // kv_slots
    rows = steps * heads
    pool_pages = kv_rows.shape[1] // (page_len * kv_slots)
    chunks = divisor_near(pool_pages, 16)
    together = divisor_near(requests, 4)
    shaped = query.reshape(requests, rows, hd)
    out = pl.pallas_call(
        functools.partial(attend_kernel, page_len, kv_slots, group, steps, chunks, together),
        out_shape=jax.ShapeDtypeStruct((requests, rows, hd), query.dtype),
        in_specs=[
            pl.BlockSpec(memory_space=pltpu.SMEM),
            pl.BlockSpec(memory_space=pltpu.VMEM),
            pl.BlockSpec(memory_space=pl.ANY),
        ],
        out_specs=pl.BlockSpec(memory_space=pltpu.VMEM),
        scratch_shapes=[
            pltpu.VMEM(kv_rows.shape, kv_rows.dtype),
            pltpu.SMEM((requests,), jnp.int32),
            pltpu.SemaphoreType.DMA((2, chunks)),
        ],
        compiler_params=pltpu.CompilerParams(vmem_limit_bytes=VMEM_BYTES),
        cost_estimate=pl.CostEstimate(
            flops=4 * requests * rows * MAXP * page_len * kv_slots * hd,
            bytes_accessed=2 * kv_rows.size,
            transcendentals=0,
        ),
        name="paged_attention",
    )(ctx_len, shaped, kv_rows)
    return out.reshape(requests * steps, width)


def project_kernel(
    count, chunks, slots, lag,
    a_ref, w_ref, out_ref,
    w_buf, own, staged, from_left, from_right,
    w_sem, send_left, send_right, recv_left, recv_right, cast_left, cast_right, cast_in,
):
    me = lax.axis_index("tp")
    width = w_buf.shape[2]
    has_left = me > 0
    has_right = me < count - 1
    left = jnp.maximum(me - 1, 0)
    right = jnp.minimum(me + 1, count - 1)

    def weights_copy(c):
        slot = lax.rem(c, slots)
        part = pl.ds(pl.multiple_of(c * width, width), width)
        return pltpu.make_async_copy(w_ref.at[:, part], w_buf.at[slot], w_sem.at[slot])

    def columns(c):
        return pl.ds(pl.multiple_of(c * width, width), width)

    def owner_of(c):
        return count // 2 - 1 + lax.rem(c, 2)

    def reduce_right(c):
        return pltpu.make_async_remote_copy(
            src_ref=staged.at[c], dst_ref=from_left.at[c],
            send_sem=send_right.at[c], recv_sem=recv_left.at[c],
            device_id={"tp": right}, device_id_type=MESH,
        )

    def reduce_left(c):
        return pltpu.make_async_remote_copy(
            src_ref=staged.at[c], dst_ref=from_right.at[c],
            send_sem=send_left.at[c], recv_sem=recv_right.at[c],
            device_id={"tp": left}, device_id_type=MESH,
        )

    def cast_to_right(c):
        return pltpu.make_async_remote_copy(
            src_ref=out_ref.at[:, columns(c)], dst_ref=out_ref.at[:, columns(c)],
            send_sem=cast_right.at[c], recv_sem=cast_in.at[c],
            device_id={"tp": right}, device_id_type=MESH,
        )

    def cast_to_left(c):
        return pltpu.make_async_remote_copy(
            src_ref=out_ref.at[:, columns(c)], dst_ref=out_ref.at[:, columns(c)],
            send_sem=cast_left.at[c], recv_sem=cast_in.at[c],
            device_id={"tp": left}, device_id_type=MESH,
        )

    for c in range(slots):
        weights_copy(c).start()

    barrier = pltpu.get_barrier_semaphore()

    @pl.when(has_left)
    def _():
        pl.semaphore_signal(barrier, inc=1, device_id={"tp": left}, device_id_type=MESH)

    @pl.when(has_right)
    def _():
        pl.semaphore_signal(barrier, inc=1, device_id={"tp": right}, device_id_type=MESH)

    pl.semaphore_wait(barrier, has_left.astype(jnp.int32) + has_right.astype(jnp.int32))

    def forward(c):
        owner = owner_of(c)

        @pl.when(me < owner)
        def _():
            cast_to_right(c).wait_recv()

            @pl.when(has_left)
            def _():
                cast_to_left(c).start()

        @pl.when(me > owner)
        def _():
            cast_to_left(c).wait_recv()

            @pl.when(has_right)
            def _():
                cast_to_right(c).start()

    edge = jnp.logical_not(has_left & has_right)

    def send_on(c):
        @pl.when(me < owner_of(c))
        def _():
            reduce_right(c).start()

        @pl.when(me > owner_of(c))
        def _():
            reduce_left(c).start()

    def compute(c):
        slot = lax.rem(c, slots)
        weights_copy(c).wait()
        own[c] = jnp.dot(a_ref[...], w_buf[slot], preferred_element_type=jnp.float32)

        @pl.when(c + slots < chunks)
        def _():
            weights_copy(c + slots).start()

        @pl.when(edge & (me != owner_of(c)))
        def _():
            staged[c] = own[c].astype(staged.dtype)
            send_on(c)

    def relay(c):
        @pl.when(jnp.logical_not(edge) & (me < owner_of(c)))
        def _():
            reduce_right(c).wait_recv()
            staged[c] = (own[c] + from_left[c].astype(jnp.float32)).astype(staged.dtype)

        @pl.when(jnp.logical_not(edge) & (me > owner_of(c)))
        def _():
            reduce_left(c).wait_recv()
            staged[c] = (own[c] + from_right[c].astype(jnp.float32)).astype(staged.dtype)

        @pl.when(jnp.logical_not(edge))
        def _():
            send_on(c)

    def finalize(c):
        @pl.when(me == owner_of(c))
        def _():
            @pl.when(has_left)
            def _():
                reduce_right(c).wait_recv()
                own[c] = own[c] + from_left[c].astype(jnp.float32)

            @pl.when(has_right)
            def _():
                reduce_left(c).wait_recv()
                own[c] = own[c] + from_right[c].astype(jnp.float32)

            out_ref[:, columns(c)] = own[c].astype(out_ref.dtype)

            @pl.when(has_left)
            def _():
                cast_to_left(c).start()

            @pl.when(has_right)
            def _():
                cast_to_right(c).start()

    def step(t, carry):
        for stage, late in ((compute, 0), (relay, 1), (finalize, 3), (forward, lag)):
            @pl.when((t >= late) & (t < chunks + late))
            def _():
                stage(t - late)

        return carry

    lax.fori_loop(0, chunks + lag, step, 0)

    def finish(c, carry):
        owner = owner_of(c)

        @pl.when(me < owner)
        def _():
            reduce_right(c).wait_send()

        @pl.when(me > owner)
        def _():
            reduce_left(c).wait_send()

        @pl.when(has_left & (me <= owner))
        def _():
            cast_to_left(c).wait_send()

        @pl.when(has_right & (me >= owner))
        def _():
            cast_to_right(c).wait_send()

        return carry

    lax.fori_loop(0, chunks, finish, 0)


def project(attention, weight, count):
    rows, depth = attention.shape
    columns = weight.shape[1]
    width = 512 if columns % 512 == 0 else 128
    chunks = columns // width
    slots = min(4, chunks)
    lag = 6
    dma = pltpu.SemaphoreType.DMA
    return pl.pallas_call(
        functools.partial(project_kernel, count, chunks, slots, lag),
        out_shape=jax.ShapeDtypeStruct((rows, columns), attention.dtype),
        in_specs=[pl.BlockSpec(memory_space=pltpu.VMEM), pl.BlockSpec(memory_space=pl.ANY)],
        out_specs=pl.BlockSpec(memory_space=pltpu.VMEM),
        scratch_shapes=[
            pltpu.VMEM((slots, depth, width), weight.dtype),
            pltpu.VMEM((chunks, rows, width), jnp.float32),
            pltpu.VMEM((chunks, rows, width), attention.dtype),
            pltpu.VMEM((chunks, rows, width), attention.dtype),
            pltpu.VMEM((chunks, rows, width), attention.dtype),
            dma((slots,)),
        ]
        + [dma((chunks,))] * 7,
        compiler_params=pltpu.CompilerParams(
            collective_id=0, has_side_effects=True, vmem_limit_bytes=VMEM_BYTES
        ),
        cost_estimate=pl.CostEstimate(
            flops=2 * rows * depth * columns,
            bytes_accessed=2 * weight.size + 100 * 1000 * 1000,
            transcendentals=0,
        ),
        name="project_and_sum",
    )(attention, weight)


def on_device(query, kv_pool, ctx_len, migrations, o_weight):
    _, pool_size, page_len, kv_slots, hd = kv_pool.shape
    slot_count, step_count, _ = query.shape
    replicas = lax.axis_size("rep")
    count = lax.axis_size("tp")
    page_rows = page_len * kv_slots
    kv_rows = kv_pool.reshape(2, pool_size * page_rows, hd)
    lists = lax.all_gather(migrations[0, 0, 1:], "rep", axis=0)
    sends = lists[:, 1] > 0
    places = jnp.arange(replicas, dtype=jnp.int32)
    shift = jnp.max(jnp.where(sends, lists[:, 0] ^ places, 0))
    outgoing = gather_pages(kv_rows, ctx_len, migrations, page_len, page_rows)
    outgoing, shift = lax.optimization_barrier((outgoing, shift))
    far = [lax.ppermute(block, "rep", [(i, i ^ 2) for i in range(replicas)]) for block in outgoing]
    attention = attend(kv_rows, ctx_len, query, page_len, kv_slots)
    layer_out = project(attention, o_weight, count)
    far, layer_out = lax.optimization_barrier((far, layer_out))
    turned = [jnp.where(shift == 1, block, crossed) for block, crossed in zip(outgoing, far)]
    near = [lax.ppermute(block, "rep", [(i, i ^ 1) for i in range(replicas)]) for block in turned]
    source = jnp.where(migrations[0, 0, 2] > 0, 0, jnp.where(shift == 2, 1, 2))
    landed = assemble(source.reshape(1), far, near)
    arrived = landed.reshape(2, -1, page_len, kv_slots, hd)
    return (layer_out.reshape(slot_count, step_count, -1), arrived)


def assemble_kernel(parts, source_ref, far0, far1, near0, near1, out_ref, held, in_sems, out_sems):
    span = held.shape[2]
    source = source_ref[0]

    def fetch(block, c, e):
        return pltpu.make_async_copy(
            block.at[pl.ds(e * span, span)], held.at[c, e], in_sems.at[c, e]
        )

    def store(c, e):
        return pltpu.make_async_copy(
            held.at[c, e], out_ref.at[c, pl.ds(e * span, span)], out_sems.at[c, e]
        )

    for c, (straight, turned) in enumerate(((far0, near0), (far1, near1))):
        for e in range(parts):
            @pl.when(source != 2)
            def _():
                fetch(straight, c, e).start()

            @pl.when(source == 2)
            def _():
                fetch(turned, c, e).start()

    for c in range(2):
        for e in range(parts):
            fetch(far0, c, e).wait()

            @pl.when(source == 0)
            def _():
                held[c, e] = jnp.zeros(held.shape[2:], held.dtype)

            store(c, e).start()
    for c in range(2):
        for e in range(parts):
            store(c, e).wait()


def assemble(source, far, near):
    rows, hd = far[0].shape
    parts = 8
    return pl.pallas_call(
        functools.partial(assemble_kernel, parts),
        out_shape=jax.ShapeDtypeStruct((2, rows, hd), far[0].dtype),
        in_specs=[pl.BlockSpec(memory_space=pltpu.SMEM)] + [pl.BlockSpec(memory_space=pl.ANY)] * 4,
        out_specs=pl.BlockSpec(memory_space=pl.ANY),
        scratch_shapes=[
            pltpu.VMEM((2, parts, rows // parts, hd), far[0].dtype),
            pltpu.SemaphoreType.DMA((2, parts)),
            pltpu.SemaphoreType.DMA((2, parts)),
        ],
        compiler_params=pltpu.CompilerParams(vmem_limit_bytes=VMEM_BYTES),
        name="assemble",
    )(source, *far, *near)


def solution(mesh):
    return jax.shard_map(
        on_device,
        mesh=mesh,
        in_specs=(
            P(("grp", "rep"), None, "tp"),
            P(None, ("grp", "rep"), None, "tp", None),
            P(("grp", "rep")),
            P(("grp", "rep"), None, None),
            P("tp", None),
        ),
        out_specs=(P(("grp", "rep"), None, None), P(None, ("grp", "rep"), None, "tp", None)),
        check_vma=False,
    )
```

profile of v0, /device:TPU:0, one launch (start us, length us, event | category | flops | bytes accessed | tf_op | source)
XLA Modules:
  0.0 139.7 jit_solution(10971675052343258462)
XLA Ops:
  0.6 0.8 copy.9.mig_ref
  1.4 0.0 copy-start.4
  1.4 0.1 slice.12
  1.5 5.9 %all-gather = s32[4,1,2]{2,1,0:T(1,128)S(1)} all-gather(s32[1,1,2]{2,1,0:T(1,128)S(1)} %slice.12), channel_id=2, replica_groups=mesh['grp'=2,'rep'=4,'tp'=4] {'rep'}, dimensions={0}, use_global_device_ids=true | all-gather | bytes 40 | tf_op jit(solution)/shard_map/all_gather | solution.py:416
  7.4 0.1 copy.11
  7.5 0.7 fusion
  8.2 0.0 copy-done.4
  8.2 0.0 copy-start.3
  8.2 6.4 %gather_pages.1 = (bf16[8192,128]{1,0:T(8,128)(2,1)}, bf16[8192,128]{1,0:T(8,128)(2,1)}) custom-call(s32[64]{0:T(128)} %ctx_ref.3, s32[1,8,3]{2,1,0:T(8,128)} %copy-done.4, bf16[2,40960,128]{2,1,0:T(8,128)(2,1)} %bitcast.13), custom_call_target="tpu_custom_call" | custom-call | tf_op jit(solution)/shard_map/gather_pages/pallas_call | solution.py:70
  14.6 1.8 %collective-permute-start = (bf16[8192,128]{1,0:T(8,128)(2,1)}, bf16[8192,128]{1,0:T(8,128)(2,1)S(1)}, u32[]{:S(2)}, u32[]{:S(2)}) collective-permute-start(bf16[8192,128]{1,0:T(8,128)(2,1)} %get-tuple-element.12), channel_id=1, source_target_pairs={{0,8},{4,12},{8,0},{12,4},{1,9},{5,13},{9,1},{13,5},{2,10},{6,14},... | collective-permute-start | bytes 6291464 | tf_op jit(solution)/shard_map/ppermute | solution.py:422
  16.5 0.3 collective-permute-start.1
  16.7 0.0 copy-done.3
  16.7 1.1 reshape.27.q_ref
  17.9 26.2 %paged_attention.1 = bf16[64,32,128]{2,1,0:T(8,128)(2,1)} custom-call(s32[64]{0:T(128)} %ctx_ref.3, bf16[64,32,128]{2,1,0:T(8,128)(2,1)} %reshape.27.q_ref, bf16[2,40960,128]{2,1,0:T(8,128)(2,1)} %bitcast.14), custom_call_target="tpu_custom_call" | custom-call | flops 1073741824 | bytes 20971520 | tf_op jit(solution)/shard_map/paged_attention/pallas_call | solution.py:167
  44.1 2.1 %reshape.28.a_ref = bf16[128,2048]{1,0:T(8,128)(2,1)} reshape(bf16[64,32,128]{2,1,0:T(8,128)(2,1)} %paged_attention.1) | data formatting | bytes 1048576 | tf_op jit(solution)/shard_map/reshape | solution.py:189
  46.8 74.1 %project_and_sum.1 = bf16[128,8192]{1,0:T(8,128)(2,1)} custom-call(bf16[128,2048]{1,0:T(8,128)(2,1)} %reshape.28.a_ref, bf16[2048,8192]{1,0:T(8,128)(2,1)} %w_ref.1), custom_call_target="tpu_custom_call" | custom-call | flops 4294967296 | bytes 133554432 | tf_op jit(solution)/shard_map/project_and_sum/pallas_call | solution.py:383
  121.0 0.0 copy-start.2
  121.0 0.0 collective-permute-done.far0
  121.0 0.0 copy-start
  121.0 0.0 collective-permute-done.1.far1
  121.0 1.6 %broadcast_select_fusion.1 = bf16[8192,128]{1,0:T(8,128)(2,1)} fusion(bf16[8192,128]{1,0:T(8,128)(2,1)} %get-tuple-element.12, bf16[8192,128]{1,0:T(8,128)(2,1)S(1)} %collective-permute-done.far0, pred[]{:T(512)S(6)} %eq.8), kind=kLoop, calls=%fused_computation.1 | loop fusion | flops 1048576 | bytes 6291457 | tf_op jit(solution)/shard_map/jit(_where)/select_n | solution.py:426
  122.6 0.5 copy-done
  123.1 0.9 copy-done.2
  124.0 3.1 %broadcast_select_fusion = bf16[8192,128]{1,0:T(8,128)(2,1)} fusion(bf16[8192,128]{1,0:T(8,128)(2,1)S(1)} %copy-done.2, bf16[8192,128]{1,0:T(8,128)(2,1)} %collective-permute-done.1.far1, pred[]{:T(512)S(6)} %eq.8), kind=kLoop, calls=%fused_computation | loop fusion | flops 1048576 | bytes 6291457 | tf_op jit(solution)/shard_map/jit(_where)/select_n | solution.py:426
  127.2 0.0 collective-permute-start.3
  127.2 0.5 collective-permute-start.2
  127.7 1.2 slice.15
  130.2 4.4 %reshape.29 = bf16[64,2,8192]{2,1,0:T(2,128)(2,1)} reshape(bf16[128,8192]{1,0:T(8,128)(2,1)} %project_and_sum.1) | data formatting | bytes 4194304 | tf_op jit(solution)/shard_map/reshape | solution.py:431
  134.6 0.0 collective-permute-done.3.near1
  134.6 0.0 copy-start.1
  134.6 0.1 collective-permute-done.2.near0
  134.7 1.3 copy-done.1
  135.9 3.8 %assemble.1 = bf16[2,8192,128]{2,1,0:T(8,128)(2,1)} custom-call(s32[1]{0:T(128)} %bitcast.5.source_ref, bf16[8192,128]{1,0:T(8,128)(2,1)} %copy-done, bf16[8192,128]{1,0:T(8,128)(2,1)} %collective-permute-done.1.far1, bf16[8192,128]{1,0:T(8,128)(2,1)} %collective-permute-done.2.near0, bf16[8192,128]{1,0:T(8,128)(2,1)} %copy-done.1), custom_call_target="tpu_custom_call" | custom-call | tf_op jit(solution)/shard_map/assemble/pallas_call | solution.py:475
Async XLA Ops:
  1.4 6.8 %copy-start.4 = (s32[1,8,3]{2,1,0:T(8,128)}, s32[1,8,3]{2,1,0:T(8,128)S(1)}, u32[]{:S(2)}) copy-start(s32[1,8,3]{2,1,0:T(8,128)S(1)} %copy.9.mig_ref) | copy-start | bytes 292
  8.2 8.5 %copy-start.3 = (bf16[64,2,2048]{2,1,0:T(2,128)(2,1)S(1)}, bf16[64,2,2048]{2,1,0:T(2,128)(2,1)}, u32[]{:S(2)}) copy-start(bf16[64,2,2048]{2,1,0:T(2,128)(2,1)} %param.5) | copy-start | bytes 1572868
  14.6 106.3 %collective-permute-start = (bf16[8192,128]{1,0:T(8,128)(2,1)}, bf16[8192,128]{1,0:T(8,128)(2,1)S(1)}, u32[]{:S(2)}, u32[]{:S(2)}) collective-permute-start(bf16[8192,128]{1,0:T(8,128)(2,1)} %get-tuple-element.12), channel_id=1, source_target_pairs={{0,8},{4,12},{8,0},{12,4},{1,9},{5,13},{9,1},{13,5},{2,10},{6,14},... | collective-permute-start | bytes 6291464 | tf_op jit(solution)/shard_map/ppermute | solution.py:422
  16.5 104.5 %collective-permute-start.1 = (bf16[8192,128]{1,0:T(8,128)(2,1)}, bf16[8192,128]{1,0:T(8,128)(2,1)}, u32[]{:S(2)}, u32[]{:S(2)}) collective-permute-start(bf16[8192,128]{1,0:T(8,128)(2,1)} %get-tuple-element.13), channel_id=1, source_target_pairs={{0,8},{4,12},{8,0},{12,4},{1,9},{5,13},{9,1},{13,5},{2,10},{6,14},... | collective-permute-start | bytes 6291464 | tf_op jit(solution)/shard_map/ppermute | solution.py:422
  121.0 3.1 %copy-start.2 = (bf16[8192,128]{1,0:T(8,128)(2,1)S(1)}, bf16[8192,128]{1,0:T(8,128)(2,1)}, u32[]{:S(2)}) copy-start(bf16[8192,128]{1,0:T(8,128)(2,1)} %get-tuple-element.13) | copy-start | bytes 6291460
  121.0 2.1 %copy-start = (bf16[8192,128]{1,0:T(8,128)(2,1)}, bf16[8192,128]{1,0:T(8,128)(2,1)S(1)}, u32[]{:S(2)}) copy-start(bf16[8192,128]{1,0:T(8,128)(2,1)S(1)} %collective-permute-done.far0) | copy-start | bytes 6291460
  127.2 7.4 %collective-permute-start.3 = (bf16[8192,128]{1,0:T(8,128)(2,1)}, bf16[8192,128]{1,0:T(8,128)(2,1)S(1)}, u32[]{:S(2)}, u32[]{:S(2)}) collective-permute-start(bf16[8192,128]{1,0:T(8,128)(2,1)} %broadcast_select_fusion), channel_id=1, source_target_pairs={{0,4},{4,0},{8,12},{12,8},{1,5},{5,1},{9,13},{13,9},{2,6},{6,2},{1... | collective-permute-start | bytes 6291464 | tf_op jit(solution)/shard_map/ppermute | solution.py:427
  127.2 7.5 %collective-permute-start.2 = (bf16[8192,128]{1,0:T(8,128)(2,1)}, bf16[8192,128]{1,0:T(8,128)(2,1)}, u32[]{:S(2)}, u32[]{:S(2)}) collective-permute-start(bf16[8192,128]{1,0:T(8,128)(2,1)} %broadcast_select_fusion.1), channel_id=1, source_target_pairs={{0,4},{4,0},{8,12},{12,8},{1,5},{5,1},{9,13},{13,9},{2,6},{6,2},{1... | collective-permute-start | bytes 6291464 | tf_op jit(solution)/shard_map/ppermute | solution.py:427
  134.6 1.4 copy-start.1
where the time goes:
time: 141 us; the launch traced here: 140 us
  Pallas kernels  111 us (79%)
  local copies, waits for them, and re-layouts  12.4 us (9%)
  blocking collectives  5.94 us (4%)
  other arithmetic  5.43 us (4%)
  between operations  2.74 us (2%)
  starting transfers between devices  2.6 us (2%)
    pallas_call x1, Pallas kernels, project(): pl.pallas_call(functools.partial(project_kernel, count, chunks, slots, la...  74.1 us
    pallas_call x1, Pallas kernels, attend(): pl.pallas_call(functools.partial(attend_kernel, page_len, kv_slots, group...  26.2 us
    pallas_call x1, Pallas kernels, gather_pages(): pl.pallas_call(functools.partial(gather_kernel, page_len, page_rows), out...  6.42 us
    all_gather x1, blocking collectives, on_device(): lists = lax.all_gather(migrations[0, 0, 1:], 'rep', axis=0)  5.94 us
    select_n x2, other arithmetic, on_device(): jnp.where(shift == 1, block, crossed)  4.71 us
    reshape x1, local copies, waits for them, and re-layouts, on_device(): return (layer_out.reshape(slot_count, step_count, -1), arrived)  4.38 us
    pallas_call x1, Pallas kernels, assemble(): pl.pallas_call(functools.partial(assemble_kernel, parts), out_shape=jax.S...  3.79 us
    unnamed x11, local copies, waits for them, and re-layouts  3.5 us
  transfers between devices with their start and end apart: 4, of which 1 were waited for; matrix products, arithmetic and copies ran while one was open for 6% of the time, Pallas kernels for 72%

commit v1 on v0

--- a/solution.py
+++ b/solution.py
@@ -413,10 +413,12 @@
     count = lax.axis_size("tp")
     page_rows = page_len * kv_slots
     kv_rows = kv_pool.reshape(2, pool_size * page_rows, hd)
-    lists = lax.all_gather(migrations[0, 0, 1:], "rep", axis=0)
-    sends = lists[:, 1] > 0
-    places = jnp.arange(replicas, dtype=jnp.int32)
-    shift = jnp.max(jnp.where(sends, lists[:, 0] ^ places, 0))
+    own = lax.axis_index("rep")
+    shift = jnp.where(migrations[0, 0, 2] > 0, migrations[0, 0, 1] ^ own, 0).reshape(1, 1)
+    for hop in (2, 1):
+        other = lax.ppermute(shift, "rep", [(i, i ^ hop) for i in range(replicas)])
+        shift = jnp.maximum(shift, other)
+    shift = shift[0, 0]
     outgoing = gather_pages(kv_rows, ctx_len, migrations, page_len, page_rows)
     outgoing, shift = lax.optimization_barrier((outgoing, shift))
     far = [lax.ppermute(block, "rep", [(i, i ^ 2) for i in range(replicas)]) for block in outgoing]

time: 141 us -> 141 us (level)
  blocking collectives: 5.94 us -> 0 us
  starting transfers between devices: 2.6 us -> 7.79 us
  waiting for transfers between devices: 0.1 us -> 2.89 us
  Pallas kernels: 111 us -> 109 us
    all_gather x1 -> x0, blocking collectives: 5.94 us -> none  [on_device(): lists = lax.all_gather(migrations[0, 0, 1:], 'rep', axis=0)]
    ppermute x0 -> x2, starting transfers between devices: none -> 5.19 us  [on_device(): other = lax.ppermute(shift, 'rep', [(i, i ^ hop) for i in range(replicas)])]
    ppermute x2, waiting for transfers between devices: 0.09 us -> 2.61 us  [on_device(): lax.ppermute(block, 'rep', [(i, i ^ 1) for i in range(replicas)])]
    unnamed x11 -> x9, local copies, waits for them, and re-layouts: 3.5 us -> 3.63 us
  transfers between devices with their start and end apart: 4 -> 6, of which waited for: 1 -> 3; matrix products, arithmetic and copies ran while one was open for 6% -> 6% of each run, Pallas kernels for 72% -> 75%
where the time goes in v1:
time: 141 us; the launch traced here: 140 us
  Pallas kernels  109 us (77%)
  local copies, waits for them, and re-layouts  12.4 us (9%)
  starting transfers between devices  7.79 us (6%)
  other arithmetic  4.73 us (3%)
  between operations  3.21 us (2%)
  waiting for transfers between devices  2.89 us (2%)
    pallas_call x1, Pallas kernels, project(): pl.pallas_call(functools.partial(project_kernel, count, chunks, slots, la...  73 us
    pallas_call x1, Pallas kernels, attend(): pl.pallas_call(functools.partial(attend_kernel, page_len, kv_slots, group...  26.6 us
    pallas_call x1, Pallas kernels, gather_pages(): pl.pallas_call(functools.partial(gather_kernel, page_len, page_rows), out...  6.07 us
    ppermute x2, starting transfers between devices, on_device(): other = lax.ppermute(shift, 'rep', [(i, i ^ hop) for i in range(replicas)])  5.19 us
    select_n x2, other arithmetic, on_device(): jnp.where(shift == 1, block, crossed)  4.73 us
    reshape x1, local copies, waits for them, and re-layouts, on_device(): return (layer_out.reshape(slot_count, step_count, -1), arrived)  4.38 us
    pallas_call x1, Pallas kernels, assemble(): pl.pallas_call(functools.partial(assemble_kernel, parts), out_shape=jax.S...  3.79 us
    unnamed x9, local copies, waits for them, and re-layouts  3.63 us
  transfers between devices with their start and end apart: 6, of which 3 were waited for; matrix products, arithmetic and copies ran while one was open for 6% of the time, Pallas kernels for 75%

profile of v1, /device:TPU:0, one launch (start us, length us, event | category | flops | bytes accessed | tf_op | source)
XLA Modules:
  0.0 140.5 jit_solution(2725407809832032932)
XLA Ops:
  0.6 1.2 fusion
  3.1 4.3 %collective-permute-start = (s32[1,1]{1,0:T(1,128)}, s32[1,1]{1,0:T(1,128)}, u32[]{:S(2)}, u32[]{:S(2)}) collective-permute-start(s32[1,1]{1,0:T(1,128)} %bitcast.3), channel_id=1, source_target_pairs={{0,8},{4,12},{8,0},{12,4},{1,9},{5,13},{9,1},{13,5},{2,10},{6,14},... | collective-permute-start | bytes 20 | tf_op jit(solution)/shard_map/ppermute | solution.py:419
  7.4 1.3 copy.7.mig_ref
  8.8 0.0 copy-start.3
  8.8 6.1 %gather_pages.1 = (bf16[8192,128]{1,0:T(8,128)(2,1)}, bf16[8192,128]{1,0:T(8,128)(2,1)}) custom-call(s32[64]{0:T(128)} %ctx_ref.3, s32[1,8,3]{2,1,0:T(8,128)} %copy.7.mig_ref, bf16[2,40960,128]{2,1,0:T(8,128)(2,1)} %bitcast.7), custom_call_target="tpu_custom_call" | custom-call | tf_op jit(solution)/shard_map/gather_pages/pallas_call | solution.py:70
  14.8 0.0 collective-permute-done
  15.4 0.9 collective-permute-start.1
  16.3 0.3 collective-permute-done.1
  17.2 0.3 collective-permute-start.2
  17.5 1.8 %collective-permute-start.3 = (bf16[8192,128]{1,0:T(8,128)(2,1)}, bf16[8192,128]{1,0:T(8,128)(2,1)}, u32[]{:S(2)}, u32[]{:S(2)}) collective-permute-start(bf16[8192,128]{1,0:T(8,128)(2,1)} %get-tuple-element.13), channel_id=1, source_target_pairs={{0,8},{4,12},{8,0},{12,4},{1,9},{5,13},{9,1},{13,5},{2,10},{6,14},... | collective-permute-start | bytes 6291464 | tf_op jit(solution)/shard_map/ppermute | solution.py:424
  19.3 0.0 copy-done.3
  19.3 1.1 reshape.29.q_ref
  20.4 26.6 %paged_attention.1 = bf16[64,32,128]{2,1,0:T(8,128)(2,1)} custom-call(s32[64]{0:T(128)} %ctx_ref.3, bf16[64,32,128]{2,1,0:T(8,128)(2,1)} %reshape.29.q_ref, bf16[2,40960,128]{2,1,0:T(8,128)(2,1)} %bitcast.8), custom_call_target="tpu_custom_call" | custom-call | flops 1073741824 | bytes 20971520 | tf_op jit(solution)/shard_map/paged_attention/pallas_call | solution.py:167
  47.0 2.1 %reshape.30.a_ref = bf16[128,2048]{1,0:T(8,128)(2,1)} reshape(bf16[64,32,128]{2,1,0:T(8,128)(2,1)} %paged_attention.1) | data formatting | bytes 1048576 | tf_op jit(solution)/shard_map/reshape | solution.py:189
  49.1 73.0 %project_and_sum.1 = bf16[128,8192]{1,0:T(8,128)(2,1)} custom-call(bf16[128,2048]{1,0:T(8,128)(2,1)} %reshape.30.a_ref, bf16[2048,8192]{1,0:T(8,128)(2,1)} %w_ref.1), custom_call_target="tpu_custom_call" | custom-call | flops 4294967296 | bytes 133554432 | tf_op jit(solution)/shard_map/project_and_sum/pallas_call | solution.py:383
  122.1 0.0 copy-start.1
  122.1 0.0 collective-permute-done.2.far0
  122.2 0.0 copy-start
  122.2 0.0 collective-permute-done.3.far1
  122.2 1.6 %broadcast_select_fusion.1 = bf16[8192,128]{1,0:T(8,128)(2,1)} fusion(bf16[8192,128]{1,0:T(8,128)(2,1)} %get-tuple-element.12, bf16[8192,128]{1,0:T(8,128)(2,1)S(1)} %collective-permute-done.2.far0, pred[]{:T(512)S(6)} %eq.8), kind=kLoop, calls=%fused_computation.1 | loop fusion | flops 1048576 | bytes 6291457 | tf_op jit(solution)/shard_map/jit(_where)/select_n | solution.py:428
  123.8 0.5 copy-done
  124.3 0.9 copy-done.1
  125.2 3.1 %broadcast_select_fusion = bf16[8192,128]{1,0:T(8,128)(2,1)} fusion(bf16[8192,128]{1,0:T(8,128)(2,1)S(1)} %copy-done.1, bf16[8192,128]{1,0:T(8,128)(2,1)} %collective-permute-done.3.far1, pred[]{:T(512)S(6)} %eq.8), kind=kLoop, calls=%fused_computation | loop fusion | flops 1048576 | bytes 6291457 | tf_op jit(solution)/shard_map/jit(_where)/select_n | solution.py:428
  128.3 0.0 collective-permute-start.5
  128.3 0.5 collective-permute-start.4
  128.9 4.4 %reshape.31 = bf16[64,2,8192]{2,1,0:T(2,128)(2,1)} reshape(bf16[128,8192]{1,0:T(8,128)(2,1)} %project_and_sum.1) | data formatting | bytes 4194304 | tf_op jit(solution)/shard_map/reshape | solution.py:433
  133.2 2.1 %collective-permute-done.5.near1 = bf16[8192,128]{1,0:T(8,128)(2,1)S(1)} collective-permute-done((bf16[8192,128]{1,0:T(8,128)(2,1)}, bf16[8192,128]{1,0:T(8,128)(2,1)S(1)}, u32[]{:S(2)}, u32[]{:S(2)}) %collective-permute-start.5) | collective-permute-done | bytes 2097184 | tf_op jit(solution)/shard_map/ppermute | solution.py:429
  135.3 0.0 copy-start.2
  135.4 0.5 collective-permute-done.4.near0
  135.8 0.8 copy-done.2
  136.7 3.8 %assemble.1 = bf16[2,8192,128]{2,1,0:T(8,128)(2,1)} custom-call(s32[1]{0:T(128)} %bitcast.5.source_ref, bf16[8192,128]{1,0:T(8,128)(2,1)} %copy-done, bf16[8192,128]{1,0:T(8,128)(2,1)} %collective-permute-done.3.far1, bf16[8192,128]{1,0:T(8,128)(2,1)} %collective-permute-done.4.near0, bf16[8192,128]{1,0:T(8,128)(2,1)} %copy-done.2), custom_call_target="tpu_custom_call" | custom-call | tf_op jit(solution)/shard_map/assemble/pallas_call | solution.py:477
Async XLA Ops:
  3.1 11.7 %collective-permute-start = (s32[1,1]{1,0:T(1,128)}, s32[1,1]{1,0:T(1,128)}, u32[]{:S(2)}, u32[]{:S(2)}) collective-permute-start(s32[1,1]{1,0:T(1,128)} %bitcast.3), channel_id=1, source_target_pairs={{0,8},{4,12},{8,0},{12,4},{1,9},{5,13},{9,1},{13,5},{2,10},{6,14},... | collective-permute-start | bytes 20 | tf_op jit(solution)/shard_map/ppermute | solution.py:419
  8.8 10.5 %copy-start.3 = (bf16[64,2,2048]{2,1,0:T(2,128)(2,1)S(1)}, bf16[64,2,2048]{2,1,0:T(2,128)(2,1)}, u32[]{:S(2)}) copy-start(bf16[64,2,2048]{2,1,0:T(2,128)(2,1)} %param.5) | copy-start | bytes 1572868
  15.4 1.2 collective-permute-start.1
  17.2 104.9 %collective-permute-start.2 = (bf16[8192,128]{1,0:T(8,128)(2,1)}, bf16[8192,128]{1,0:T(8,128)(2,1)S(1)}, u32[]{:S(2)}, u32[]{:S(2)}) collective-permute-start(bf16[8192,128]{1,0:T(8,128)(2,1)} %get-tuple-element.12), channel_id=1, source_target_pairs={{0,8},{4,12},{8,0},{12,4},{1,9},{5,13},{9,1},{13,5},{2,10},{6,14},... | collective-permute-start | bytes 6291464 | tf_op jit(solution)/shard_map/ppermute | solution.py:424
  17.5 104.7 %collective-permute-start.3 = (bf16[8192,128]{1,0:T(8,128)(2,1)}, bf16[8192,128]{1,0:T(8,128)(2,1)}, u32[]{:S(2)}, u32[]{:S(2)}) collective-permute-start(bf16[8192,128]{1,0:T(8,128)(2,1)} %get-tuple-element.13), channel_id=1, source_target_pairs={{0,8},{4,12},{8,0},{12,4},{1,9},{5,13},{9,1},{13,5},{2,10},{6,14},... | collective-permute-start | bytes 6291464 | tf_op jit(solution)/shard_map/ppermute | solution.py:424
  122.1 3.1 %copy-start.1 = (bf16[8192,128]{1,0:T(8,128)(2,1)S(1)}, bf16[8192,128]{1,0:T(8,128)(2,1)}, u32[]{:S(2)}) copy-start(bf16[8192,128]{1,0:T(8,128)(2,1)} %get-tuple-element.13) | copy-start | bytes 6291460
  122.2 2.1 %copy-start = (bf16[8192,128]{1,0:T(8,128)(2,1)}, bf16[8192,128]{1,0:T(8,128)(2,1)S(1)}, u32[]{:S(2)}) copy-start(bf16[8192,128]{1,0:T(8,128)(2,1)S(1)} %collective-permute-done.2.far0) | copy-start | bytes 6291460
  128.3 7.0 %collective-permute-start.5 = (bf16[8192,128]{1,0:T(8,128)(2,1)}, bf16[8192,128]{1,0:T(8,128)(2,1)S(1)}, u32[]{:S(2)}, u32[]{:S(2)}) collective-permute-start(bf16[8192,128]{1,0:T(8,128)(2,1)} %broadcast_select_fusion), channel_id=1, source_target_pairs={{0,4},{4,0},{8,12},{12,8},{1,5},{5,1},{9,13},{13,9},{2,6},{6,2},{1... | collective-permute-start | bytes 6291464 | tf_op jit(solution)/shard_map/ppermute | solution.py:429
  128.3 7.5 %collective-permute-start.4 = (bf16[8192,128]{1,0:T(8,128)(2,1)}, bf16[8192,128]{1,0:T(8,128)(2,1)}, u32[]{:S(2)}, u32[]{:S(2)}) collective-permute-start(bf16[8192,128]{1,0:T(8,128)(2,1)} %broadcast_select_fusion.1), channel_id=1, source_target_pairs={{0,4},{4,0},{8,12},{12,8},{1,5},{5,1},{9,13},{13,9},{2,6},{6,2},{1... | collective-permute-start | bytes 6291464 | tf_op jit(solution)/shard_map/ppermute | solution.py:429
  135.3 1.3 copy-start.2
